TPU v7x, 32 devices: a whole 2x2x4 slice. The times are simulated.
32 devices in a mesh: ctx: 8 (over z, x), head: 4 (over y, core).
Axes of the slice: x: 2, y: 2, z: 4, core: 2. Of those that a mesh axis runs over, the one named last changes fastest.
Arguments:
- queries: bfloat16 [2048, 2048], P('ctx', 'head'), may hold values from -4.5 to 4.5
- key_states: bfloat16 [2048, 512], P('ctx', 'head'), may hold values from -4.5 to 4.5
- value_states: bfloat16 [2048, 512], P('ctx', 'head'), may hold values from -6 to 6
- doc_lengths: int32 [4], replicated, may hold values from 1 to 1024, 2048 in all
- out_weight: bfloat16 [4096, 2048], P('ctx', 'head'), may hold values from -0.125 to 0.125
- out_grad: bfloat16 [2048, 4096], P('ctx', 'head'), may hold values from -6 to 6
Outputs:
- projected: bfloat16 [2048, 4096], P('ctx', 'head')
- query_grad: bfloat16 [2048, 2048], P('ctx', 'head')
- key_grad: bfloat16 [2048, 512], P('ctx', 'head')
- value_grad: bfloat16 [2048, 512], P('ctx', 'head')
Inputs may be any that keep to these rules, and one draw needn't show every extreme that they name: `doc_lengths`: the lengths sum to 2048; the longest is exactly 1024.
All inputs are finite; a program needn't handle non-finite values.
Results may differ from a plain program's by a relative error of at most 0.014.
Values may be sent and summed in bfloat16 or wider, within the bound.
A program may use at most 64 MiB of HBM per device.

v0:
```python
import jax
import jax.numpy as jnp
from jax import lax
from jax.sharding import PartitionSpec as P

HEAD_DIM = 128
REACH = 4


NEGATIVE = -1e30


def shifted(value, axis, steps):
    count = lax.axis_size(axis)
    leading, last = (max(0, -steps), min(count, count - steps))
    return lax.ppermute(value, axis, [(source, source + steps) for source in range(leading, last)])


def doc_starts(doc_lengths, positions):
    doc_ends = jnp.cumsum(doc_lengths)
    passed = doc_ends[None, :] <= positions[:, None]
    return jnp.sum(jnp.where(passed, doc_lengths[None, :], 0), axis=1)


def guarded(flag, compute, empty_fn):
    return lax.cond(flag, lambda unused: compute(), lambda unused: empty_fn(), 0)


def per_device(queries, key_states, value_states, doc_lengths, out_weight, out_grad):
    row_count = queries.shape[0]
    kv_cols = key_states.shape[1]
    kv_local = kv_cols // HEAD_DIM
    group_size = queries.shape[1] // kv_cols
    score_scale = HEAD_DIM ** (-0.5)
    my_rank = lax.axis_index("ctx")
    offsets = jnp.arange(row_count, dtype=jnp.int32)
    positions = my_rank * row_count + offsets
    starts = doc_starts(doc_lengths, positions)
    head_shape = (row_count, kv_local, group_size, HEAD_DIM)
    stat_shape = (kv_local, group_size, row_count)
    query_rows = queries.reshape(head_shape)
    stacked = jnp.concatenate([key_states, value_states], axis=1)
    fetched = [stacked] + [shifted(stacked, "ctx", distance) for distance in range(1, REACH + 1)]
    blocks_info = []
    for distance in range(REACH + 1):
        owner = my_rank - distance
        key_pos = owner * row_count + offsets
        allowed = (key_pos[None, :] >= starts[:, None]) & (key_pos[None, :] <= positions[:, None])
        is_live = jnp.logical_and(owner >= 0, starts[0] < (owner + 1) * row_count)
        flag = None
        flag = is_live
        key_block = fetched[distance][:, :kv_cols].reshape(row_count, kv_local, HEAD_DIM)
        value_block = fetched[distance][:, kv_cols:].reshape(row_count, kv_local, HEAD_DIM)
        blocks_info.append((key_block, value_block, allowed, flag))

    def masked_scores(rows, key_block, allowed):
        scores = (
            jnp.einsum("tgqd,cgd->gqtc", rows, key_block, preferred_element_type=jnp.float32)
            * score_scale
        )
        return jnp.where(allowed, scores, NEGATIVE)

    def pair_stats(rows, key_block, allowed):
        masked = masked_scores(rows, key_block, allowed)
        row_max = jnp.max(masked, axis=-1)
        row_sum = jnp.sum(jnp.where(allowed, jnp.exp(masked - row_max[..., None]), 0.0), axis=-1)
        return (row_max, row_sum)

    def pair_mix(rows, key_block, value_block, allowed, totals_log):
        masked = masked_scores(rows, key_block, allowed)
        soft_probs = jnp.exp(masked - totals_log[..., None]).astype(jnp.bfloat16)
        return jnp.einsum(
            "gqtc,cgd->tgqd", soft_probs, value_block, preferred_element_type=jnp.float32
        )

    def pair_grads(rows, key_block, value_block, allowed, totals_log, grad_block, delta_block):
        masked = masked_scores(rows, key_block, allowed)
        exact_probs = jnp.exp(masked - totals_log[..., None])
        soft_probs = exact_probs.astype(jnp.bfloat16)
        grad_probs = jnp.einsum(
            "tgqd,cgd->gqtc", grad_block, value_block, preferred_element_type=jnp.float32
        )
        grad_scores = (exact_probs * (grad_probs - delta_block[..., None])).astype(jnp.bfloat16)
        query_part = jnp.einsum(
            "gqtc,cgd->tgqd", grad_scores, key_block, preferred_element_type=jnp.float32
        )
        key_part = jnp.einsum(
            "gqtc,tgqd->cgd", grad_scores, rows, preferred_element_type=jnp.float32
        )
        value_part = jnp.einsum(
            "gqtc,tgqd->cgd", soft_probs, grad_block, preferred_element_type=jnp.float32
        )
        joined = jnp.concatenate(
            [key_part.reshape(row_count, kv_cols), value_part.reshape(row_count, kv_cols)], axis=1
        )
        return (query_part, joined)

    def empty_stats():
        return (jnp.full(stat_shape, NEGATIVE, jnp.float32), jnp.zeros(stat_shape, jnp.float32))

    def empty_rows():
        return jnp.zeros(head_shape, jnp.float32)

    def empty_grads():
        return (
            jnp.zeros(head_shape, jnp.float32),
            jnp.zeros((row_count, 2 * kv_cols), jnp.float32),
        )

    maxima = []
    totals = []
    for key_block, value_block, allowed, flag in blocks_info:

        def local_stats(key_block=key_block, allowed=allowed):
            return pair_stats(query_rows, key_block, allowed)

        row_max, row_sum = guarded(flag, local_stats, empty_stats)
        maxima.append(row_max)
        totals.append(row_sum)
    overall = maxima[0]
    for row_max in maxima[1:]:
        overall = jnp.maximum(overall, row_max)
    summed = jnp.zeros(stat_shape, jnp.float32)
    for row_max, row_sum in zip(maxima, totals):
        summed = summed + row_sum * jnp.exp(row_max - overall)
    log_total = overall + jnp.log(summed)
    attended_acc = jnp.zeros(head_shape, jnp.float32)
    for key_block, value_block, allowed, flag in blocks_info:

        def local_mix(key_block=key_block, value_block=value_block, allowed=allowed):
            return pair_mix(query_rows, key_block, value_block, allowed, log_total)

        attended_acc = attended_acc + guarded(flag, local_mix, empty_rows)
    attended = attended_acc.astype(jnp.bfloat16).reshape(row_count, queries.shape[1])
    partial_out = jnp.einsum(
        "tk,ck->tc",
        attended,
        lax.all_gather(out_weight, "ctx", axis=0, tiled=True),
        preferred_element_type=jnp.float32,
    )
    projected = lax.psum_scatter(
        partial_out.astype(jnp.bfloat16), "head", scatter_dimension=1, tiled=True
    )
    full_grad = lax.all_gather(out_grad, "head", axis=1, tiled=True)
    attended_grad = jnp.dot(
        full_grad,
        lax.all_gather(out_weight, "ctx", axis=0, tiled=True),
        preferred_element_type=jnp.float32,
    )
    attended_grad = attended_grad.astype(jnp.bfloat16)
    grad_rows = attended_grad.reshape(head_shape)
    product = attended_grad.astype(jnp.float32) * attended.astype(jnp.float32)
    row_delta = jnp.sum(product.reshape(head_shape), axis=-1).transpose(1, 2, 0)
    query_acc = jnp.zeros(head_shape, jnp.float32)
    kv_parts = []
    for key_block, value_block, allowed, flag in blocks_info:

        def local_grads(key_block=key_block, value_block=value_block, allowed=allowed):
            return pair_grads(
                query_rows, key_block, value_block, allowed, log_total, grad_rows, row_delta
            )

        query_part, joined = guarded(flag, local_grads, empty_grads)
        query_acc = query_acc + query_part
        kv_parts.append(joined)
    kv_sum = kv_parts[0]
    for distance in range(1, REACH + 1):
        kv_sum = kv_sum + shifted(kv_parts[distance].astype(jnp.bfloat16), "ctx", -distance).astype(
            jnp.float32
        )
    query_grad = (query_acc * score_scale).astype(jnp.bfloat16).reshape(row_count, queries.shape[1])
    key_grad = (kv_sum[:, :kv_cols] * score_scale).astype(jnp.bfloat16)
    value_grad = kv_sum[:, kv_cols:].astype(jnp.bfloat16)
    return (projected, query_grad, key_grad, value_grad)


def solution(mesh):
    in_specs = (
        P("ctx", "head"),
        P("ctx", "head"),
        P("ctx", "head"),
        P(),
        P("ctx", "head"),
        P("ctx", "head"),
    )
    out_specs = (P("ctx", "head"), P("ctx", "head"), P("ctx", "head"), P("ctx", "head"))
    return jax.shard_map(
        per_device, mesh=mesh, in_specs=in_specs, out_specs=out_specs, check_vma=False
    )
```

profile of v0, /device:TPU:27, one launch (start us, length us, event | category | flops | bytes accessed | tf_op | source)
XLA Modules:
  0.0 164.9 jit_solution(16600088362671472461)
XLA Ops:
  8.7 0.9 constant_dynamic-update-slice_fusion.1
  9.6 0.9 constant_dynamic-update-slice_fusion
  10.4 1.3 collective-permute-start.3
  11.7 1.3 collective-permute-start.2
  13.0 1.3 collective-permute-start.1
  14.3 1.3 collective-permute-start
  19.0 1.1 copy.151
  22.5 2.7 %conditional.15 = (f32[1,4,256]{2,1,0:T(4,128)}, f32[1,4,256]{2,1,0:T(4,128)S(1)}) conditional(s32[]{:T(128)} %convert_element_type.116, () %tuple.119, (pred[256,256]{0,1:T(8,128)(4,1)S(1)}, bf16[256,1,128]{2,0,1:T(8,128)(2,1)}, bf16[256,1,4,128]{0,3,2,1:T(8,128)(2,1)S(1)}) %tuple.268), branch_computations={%region_2.3_spmd, %region_3.6_spmd} | conditional | flops 68679680 | bytes 2568208 | solution.py:26
  22.5 1.8 %fusion.193 = (f32[4,256]{1,0:T(4,128)}, f32[1,4,256,256]{2,3,1,0:T(8,128)S(1)}) fusion(bf16[256,1,4,128]{0,3,2,1:T(8,128)(2,1)S(1)} %get-tuple-element.436, bf16[256,1,128]{2,0,1:T(8,128)(2,1)} %get-tuple-element.159, pred[256,256]{0,1:T(8,128)(4,1)S(1)} %get-tuple-element.158), kind=kOutput, calls=%fused_computation.264 | convolution fusion | flops 67894272 | bytes 1445888 | tf_op jit(solution)/shard_map/cond/branch_1_fun/tgqd,cgd->gqtc/dot_general | solution.py:58
  24.3 0.9 select_reduce_fusion
  25.2 3.5 %collective-permute-done.3 = bf16[256,256]{1,0:T(8,128)(2,1)S(1)} collective-permute-done((bf16[256,256]{1,0:T(8,128)(2,1)S(1)}, bf16[256,256]{1,0:T(8,128)(2,1)S(1)}, u32[]{:S(2)}, u32[]{:S(2)}) %collective-permute-start.3) | collective-permute-done | bytes 131104 | tf_op jit(solution)/shard_map/ppermute | solution.py:16
  30.0 1.8 %conditional.18 = (f32[1,4,256]{2,1,0:T(4,128)}, f32[1,4,256]{2,1,0:T(4,128)S(1)}) conditional(s32[]{:T(128)} %convert_element_type.119, () %tuple.125, (pred[256,256]{0,1:T(8,128)(4,1)S(1)}, bf16[256,1,128]{2,0,1:T(8,128)(2,1)S(1)}, bf16[256,1,4,128]{0,3,2,1:T(8,128)(2,1)S(1)}) %tuple.250), branch_computations={%region_14.15_spmd, %region_15.18_spmd} | conditional | flops 68679680 | bytes 2568208 | solution.py:26
  30.0 0.9 fusion.196
  30.9 0.9 select_reduce_fusion.3
  31.8 1.8 %conditional.17 = (f32[1,4,256]{2,1,0:T(4,128)}, f32[1,4,256]{2,1,0:T(4,128)S(1)}) conditional(s32[]{:T(128)} %convert_element_type.118, () %tuple.123, (pred[256,256]{0,1:T(8,128)(4,1)S(1)}, bf16[256,1,128]{2,0,1:T(8,128)(2,1)S(1)}, bf16[256,1,4,128]{0,3,2,1:T(8,128)(2,1)S(1)}) %tuple.251), branch_computations={%region_10.11_spmd, %region_11.14_spmd} | conditional | flops 68679680 | bytes 2568208 | solution.py:26
  31.8 0.9 fusion.195
  32.7 0.9 select_reduce_fusion.2
  33.6 1.8 %conditional.16 = (f32[1,4,256]{2,1,0:T(4,128)}, f32[1,4,256]{2,1,0:T(4,128)S(1)}) conditional(s32[]{:T(128)} %convert_element_type.117, () %tuple.121, (pred[256,256]{0,1:T(8,128)(4,1)S(1)}, bf16[256,1,128]{2,0,1:T(8,128)(2,1)S(1)}, bf16[256,1,4,128]{0,3,2,1:T(8,128)(2,1)S(1)}) %tuple.252), branch_computations={%region_6.7_spmd, %region_7.10_spmd} | conditional | flops 68679680 | bytes 2568208 | solution.py:26
  33.6 0.9 fusion.194
  34.6 0.9 select_reduce_fusion.1
  38.4 1.5 conditional.21
  38.5 1.5 convolution_bitcast_fusion.1
  40.3 50.3 %all-gather.3.cloned.1.call-done = bf16[4096,512]{1,0:T(8,128)(2,1)} async-done(((bf16[512,512]{1,0:T(8,128)(2,1)}), bf16[4096,512]{1,0:T(8,128)(2,1)}) %all-gather.3.cloned.1.call-update) | async-done | bytes 4194320 | tf_op jit(solution)/shard_map/all_gather | solution.py:138
  90.6 4.8 %convolution_convert_fusion = bf16[256,4096]{1,0:T(8,128)(2,1)} fusion(bf16[4096,512]{1,0:T(8,128)(2,1)} %all-gather.3.cloned.1.call-done, bf16[32,8,4,128]{3,2,1,0:T(4,128)(2,1)S(1)} %bitcast.681), kind=kOutput, calls=%fused_computation.230 | convolution fusion | flops 1074790400 | bytes 6553600 | tf_op jit(solution)/shard_map/tk,ck->tc/dot_general | solution.py:135
  95.5 20.6 %all-gather.5.cloned.1.call-done = bf16[256,4096]{1,0:T(8,128)(2,1)} async-done(((bf16[256,1024]{1,0:T(8,128)(2,1)}), bf16[256,4096]{1,0:T(8,128)(2,1)}) %all-gather.5.cloned.1.call-update) | async-done | bytes 2097168 | tf_op jit(solution)/shard_map/all_gather | solution.py:144
  116.1 4.1 %convert_multiply_fusion = (f32[256,512]{1,0:T(8,128)S(1)}, bf16[256,512]{1,0:T(8,128)(2,1)S(1)}) fusion(bf16[32,8,4,128]{3,2,1,0:T(4,128)(2,1)S(1)} %bitcast.682, bf16[256,4096]{1,0:T(8,128)(2,1)} %all-gather.5.cloned.1.call-done, bf16[4096,512]{1,0:T(8,128)(2,1)} %all-gather.3.cloned.1.call-done), kind=kOutput, calls=%fused_computation.233 | convolution fusion | flops 1074266112 | bytes 7340032 | tf_op jit(solution)/shard_map/dot_general | solution.py:145
  121.6 2.8 %collective-permute-start.7 = (bf16[256,256]{1,0:T(8,128)(2,1)}, bf16[256,256]{1,0:T(8,128)(2,1)}, u32[]{:S(2)}, u32[]{:S(2)}) collective-permute-start(bf16[256,256]{1,0:T(8,128)(2,1)} %copy.178), channel_id=1, source_target_pairs={{16,0},{20,4},{24,8},{28,12},{17,1},{21,5},{25,9},{29,13},{18,2},{... | collective-permute-start | bytes 393224 | tf_op jit(solution)/shard_map/ppermute | solution.py:16
  124.4 2.8 %conditional.28 = (f32[256,1,4,128]{3,0,2,1:T(8,128)S(1)}, bf16[256,256]{0,1:T(8,128)(2,1)S(1)}) conditional(s32[]{:T(128)} %convert_element_type.119, () %tuple.144, (pred[256,256]{0,1:T(8,128)(4,1)S(1)}, bf16[256,1,128]{2,0,1:T(8,128)(2,1)S(1)}, bf16[256,1,4,128]{0,3,2,1:T(8,128)(2,1)S(1)}, f32[1,4,256]{2,1,0:T(4,128)S(1)}, ...), branch_computations={%region_40.41_spmd, %region_41.42_spmd} | conditional | flops 337641472 | bytes 7487504 | solution.py:26
  125.0 1.1 fusion.163
  127.9 2.0 %collective-permute-start.6 = (bf16[256,256]{1,0:T(8,128)(2,1)}, bf16[256,256]{1,0:T(8,128)(2,1)}, u32[]{:S(2)}, u32[]{:S(2)}) collective-permute-start(bf16[256,256]{1,0:T(8,128)(2,1)} %copy.177), channel_id=1, source_target_pairs={{12,0},{16,4},{20,8},{24,12},{28,16},{13,1},{17,5},{21,9},{25,13},... | collective-permute-start | bytes 393224 | tf_op jit(solution)/shard_map/ppermute | solution.py:16
  129.9 4.4 %conditional.27 = (f32[256,1,4,128]{3,0,2,1:T(8,128)S(1)}, bf16[256,256]{0,1:T(8,128)(2,1)}) conditional(s32[]{:T(128)} %convert_element_type.118, () %tuple.142, (pred[256,256]{0,1:T(8,128)(4,1)S(1)}, bf16[256,1,128]{2,0,1:T(8,128)(2,1)S(1)}, bf16[256,1,4,128]{0,3,2,1:T(8,128)(2,1)S(1)}, f32[1,4,256]{2,1,0:T(4,128)S(1)}, ...), branch_computations={%region_38.39_spmd, %region_39.40_spmd} | conditional | flops 337641472 | bytes 7749676 | solution.py:26
  130.7 1.1 fusion.146
  131.8 1.2 convolution_bitcast_fusion.14
  134.3 1.7 %copy.176 = bf16[256,256]{1,0:T(8,128)(2,1)} copy(bf16[256,256]{0,1:T(8,128)(2,1)} %get-tuple-element.281) | data formatting | bytes 262144 | tf_op jit(solution)/shard_map/cond | solution.py:26
  135.9 1.9 %collective-permute-start.5 = (bf16[256,256]{1,0:T(8,128)(2,1)}, bf16[256,256]{1,0:T(8,128)(2,1)}, u32[]{:S(2)}, u32[]{:S(2)}) collective-permute-start(bf16[256,256]{1,0:T(8,128)(2,1)} %copy.176), channel_id=1, source_target_pairs={{8,0},{12,4},{16,8},{20,12},{24,16},{28,20},{9,1},{13,5},{17,9},{2... | collective-permute-start | bytes 393224 | tf_op jit(solution)/shard_map/ppermute | solution.py:16
  137.9 5.9 %conditional.26 = (f32[256,1,4,128]{3,0,2,1:T(8,128)}, bf16[256,256]{0,1:T(8,128)(2,1)}) conditional(s32[]{:T(128)} %convert_element_type.117, () %tuple.140, (pred[256,256]{0,1:T(8,128)(4,1)}, bf16[256,1,128]{2,0,1:T(8,128)(2,1)}, bf16[256,1,4,128]{0,3,2,1:T(8,128)(2,1)S(1)}, f32[1,4,256]{2,1,0:T(4,128)S(1)}, bf16[256,1,128]{2,0,1:T(8,128)(2,1)}, ...), branch_computations={%region_36.37_spmd, %region_37.38_spmd} | conditional | flops 337641472 | bytes 7487504 | solution.py:26
  137.9 1.2 fusion.128
  139.4 1.1 fusion.129
  140.5 2.0 %convolution_bitcast_fusion.10 = f32[256,1,4,128]{3,0,2,1:T(8,128)} fusion(bf16[4,256,256]{1,2,0:T(8,128)(2,1)S(1)} %fusion.129, bf16[256,1,128]{2,0,1:T(8,128)(2,1)} %get-tuple-element.213), kind=kOutput, calls=%fused_computation.148 | convolution fusion | flops 67108864 | bytes 1114112 | tf_op jit(solution)/shard_map/cond/branch_1_fun/gqtc,cgd->tgqd/dot_general | solution.py:84
  143.8 1.7 %copy.174 = bf16[256,256]{1,0:T(8,128)(2,1)} copy(bf16[256,256]{0,1:T(8,128)(2,1)} %get-tuple-element.280) | data formatting | bytes 262144 | tf_op jit(solution)/shard_map/cond | solution.py:26
  145.5 1.9 %collective-permute-start.4 = (bf16[256,256]{1,0:T(8,128)(2,1)}, bf16[256,256]{1,0:T(8,128)(2,1)}, u32[]{:S(2)}, u32[]{:S(2)}) collective-permute-start(bf16[256,256]{1,0:T(8,128)(2,1)} %copy.174), channel_id=1, source_target_pairs={{4,0},{8,4},{12,8},{16,12},{20,16},{24,20},{28,24},{5,1},{9,5},{13... | collective-permute-start | bytes 393224 | tf_op jit(solution)/shard_map/ppermute | solution.py:16
  147.4 6.1 %conditional.25 = (f32[256,1,4,128]{3,0,2,1:T(8,128)}, f32[256,256]{1,0:T(8,128)}) conditional(s32[]{:T(128)} %convert_element_type.116, () %tuple.138, (pred[256,256]{0,1:T(8,128)(4,1)}, bf16[256,1,128]{2,0,1:T(8,128)(2,1)}, bf16[256,1,4,128]{0,3,2,1:T(8,128)(2,1)S(1)}, f32[1,4,256]{2,1,0:T(4,128)S(1)}, bf16[256,1,128]{2,0,1:T(8,128)(2,1)}, ...), branch_computations={%region_34.35_spmd, %region_35.36_spmd} | conditional | flops 337444864 | bytes 8405008 | solution.py:26
  147.4 1.2 fusion.111
  148.9 1.1 fusion.112
  150.1 2.0 %convolution_bitcast_fusion.6 = f32[256,1,4,128]{3,0,2,1:T(8,128)} fusion(bf16[4,256,256]{1,2,0:T(8,128)(2,1)S(1)} %fusion.112, bf16[256,1,128]{2,0,1:T(8,128)(2,1)} %get-tuple-element.206), kind=kOutput, calls=%fused_computation.125 | convolution fusion | flops 67108864 | bytes 1114112 | tf_op jit(solution)/shard_map/cond/branch_1_fun/gqtc,cgd->tgqd/dot_general | solution.py:84
  152.7 0.8 copy.220
  153.6 1.3 multiply_convert_fusion
  155.9 1.2 convert_add_fusion
  (94 shorter events, 21.7 us)
Async XLA Ops:
  7.2 83.5 %all-gather.3.cloned.1.call-start = ((), (), s32[]{:S(2)}) async-start(), calls=%async_computation.1 | async-start | bytes 4718592 | tf_op jit(solution)/shard_map/all_gather | solution.py:138
  7.9 108.2 %all-gather.5.cloned.1.call-start = ((), (), s32[]{:S(2)}) async-start(), calls=%async_computation.3 | async-start | bytes 2621440 | tf_op jit(solution)/shard_map/all_gather | solution.py:144
  8.6 149.7 %reduce-scatter.2.cloned.1.call-start = ((), (), s32[]{:S(2)}) async-start(), calls=%async_computation.2 | async-start | bytes 2621440 | tf_op jit(solution)/shard_map/reduce_scatter | solution.py:141
  10.4 18.2 %collective-permute-start.3 = (bf16[256,256]{1,0:T(8,128)(2,1)S(1)}, bf16[256,256]{1,0:T(8,128)(2,1)S(1)}, u32[]{:S(2)}, u32[]{:S(2)}) collective-permute-start(bf16[256,256]{1,0:T(8,128)(2,1)S(1)} %constant_dynamic-update-slice_fusion), channel_id=1, source_target_pairs={{0,16},{4,20},{8,24},{12,28},{1,17},{5,21},{9,25},{13,29},{2,18},{... | collective-permute-start | bytes 393224 | tf_op jit(solution)/shard_map/ppermute | solution.py:16
  11.7 17.0 %collective-permute-start.2 = (bf16[256,256]{1,0:T(8,128)(2,1)S(1)}, bf16[256,256]{1,0:T(8,128)(2,1)S(1)}, u32[]{:S(2)}, u32[]{:S(2)}) collective-permute-start(bf16[256,256]{1,0:T(8,128)(2,1)S(1)} %constant_dynamic-update-slice_fusion), channel_id=1, source_target_pairs={{0,12},{4,16},{8,20},{12,24},{16,28},{1,13},{5,17},{9,21},{13,25},... | collective-permute-start | bytes 393224 | tf_op jit(solution)/shard_map/ppermute | solution.py:16
  13.0 15.7 %collective-permute-start.1 = (bf16[256,256]{1,0:T(8,128)(2,1)S(1)}, bf16[256,256]{1,0:T(8,128)(2,1)S(1)}, u32[]{:S(2)}, u32[]{:S(2)}) collective-permute-start(bf16[256,256]{1,0:T(8,128)(2,1)S(1)} %constant_dynamic-update-slice_fusion), channel_id=1, source_target_pairs={{0,8},{4,12},{8,16},{12,20},{16,24},{20,28},{1,9},{5,13},{9,17},{1... | collective-permute-start | bytes 393224 | tf_op jit(solution)/shard_map/ppermute | solution.py:16
  14.3 14.4 %collective-permute-start = (bf16[256,256]{1,0:T(8,128)(2,1)S(1)}, bf16[256,256]{1,0:T(8,128)(2,1)S(1)}, u32[]{:S(2)}, u32[]{:S(2)}) collective-permute-start(bf16[256,256]{1,0:T(8,128)(2,1)S(1)} %constant_dynamic-update-slice_fusion), channel_id=1, source_target_pairs={{0,4},{4,8},{8,12},{12,16},{16,20},{20,24},{24,28},{1,5},{5,9},{9,... | collective-permute-start | bytes 393224 | tf_op jit(solution)/shard_map/ppermute | solution.py:16
  22.5 15.3 %copy-start.1 = (pred[256,256]{0,1:T(8,128)(4,1)}, pred[256,256]{0,1:T(8,128)(4,1)S(1)}, u32[]{:S(2)}) copy-start(pred[256,256]{0,1:T(8,128)(4,1)S(1)} %get-tuple-element.528) | copy-start | bytes 196612
  22.5 15.9 %copy-start.2 = (pred[256,256]{0,1:T(8,128)(4,1)}, pred[256,256]{0,1:T(8,128)(4,1)S(1)}, u32[]{:S(2)}) copy-start(pred[256,256]{0,1:T(8,128)(4,1)S(1)} %get-tuple-element.532) | copy-start | bytes 196612
  28.7 7.6 %copy-start.8 = (bf16[256,1,128]{2,0,1:T(8,128)(2,1)}, bf16[256,1,128]{2,0,1:T(8,128)(2,1)S(1)}, u32[]{:S(2)}) copy-start(bf16[256,1,128]{2,0,1:T(8,128)(2,1)S(1)} %get-tuple-element.526) | copy-start | bytes 196612
  28.7 7.6 %copy-start.7 = (bf16[256,1,128]{2,0,1:T(8,128)(2,1)}, bf16[256,1,128]{2,0,1:T(8,128)(2,1)S(1)}, u32[]{:S(2)}) copy-start(bf16[256,1,128]{2,0,1:T(8,128)(2,1)S(1)} %get-tuple-element.524) | copy-start | bytes 196612
  28.7 8.3 %copy-start.6 = (bf16[256,1,128]{2,0,1:T(8,128)(2,1)}, bf16[256,1,128]{2,0,1:T(8,128)(2,1)S(1)}, u32[]{:S(2)}) copy-start(bf16[256,1,128]{2,0,1:T(8,128)(2,1)S(1)} %get-tuple-element.522) | copy-start | bytes 196612
  29.4 9.0 %copy-start.3 = (bf16[256,1,128]{2,0,1:T(8,128)(2,1)}, bf16[256,1,128]{2,0,1:T(8,128)(2,1)S(1)}, u32[]{:S(2)}) copy-start(bf16[256,1,128]{2,0,1:T(8,128)(2,1)S(1)} %get-tuple-element.521) | copy-start | bytes 196612
  35.4 2.3 %copy-start = (bf16[256,128]{1,0:T(8,128)(2,1)S(1)}, bf16[256,128]{1,0:T(8,128)(2,1)}, u32[]{:S(2)}) copy-start(bf16[256,128]{1,0:T(8,128)(2,1)} %param.37) | copy-start | bytes 196612
  35.5 2.3 %copy-start.5 = (bf16[256,128]{1,0:T(8,128)(2,1)S(1)}, bf16[256,128]{1,0:T(8,128)(2,1)}, u32[]{:S(2)}) copy-start(bf16[256,128]{1,0:T(8,128)(2,1)} %param.38) | copy-start | bytes 196612
  95.5 25.3 %copy-start.9 = (bf16[256,1,128]{2,0,1:T(8,128)(2,1)S(1)}, bf16[256,1,128]{2,0,1:T(8,128)(2,1)}, u32[]{:S(2)}) copy-start(bf16[256,1,128]{2,0,1:T(8,128)(2,1)} %copy-done.8) | copy-start | bytes 196612
  121.6 34.2 %collective-permute-start.7 = (bf16[256,256]{1,0:T(8,128)(2,1)}, bf16[256,256]{1,0:T(8,128)(2,1)}, u32[]{:S(2)}, u32[]{:S(2)}) collective-permute-start(bf16[256,256]{1,0:T(8,128)(2,1)} %copy.178), channel_id=1, source_target_pairs={{16,0},{20,4},{24,8},{28,12},{17,1},{21,5},{25,9},{29,13},{18,2},{... | collective-permute-start | bytes 393224 | tf_op jit(solution)/shard_map/ppermute | solution.py:16
  127.9 27.9 %collective-permute-start.6 = (bf16[256,256]{1,0:T(8,128)(2,1)}, bf16[256,256]{1,0:T(8,128)(2,1)}, u32[]{:S(2)}, u32[]{:S(2)}) collective-permute-start(bf16[256,256]{1,0:T(8,128)(2,1)} %copy.177), channel_id=1, source_target_pairs={{12,0},{16,4},{20,8},{24,12},{28,16},{13,1},{17,5},{21,9},{25,13},... | collective-permute-start | bytes 393224 | tf_op jit(solution)/shard_map/ppermute | solution.py:16
  129.9 0.6 copy-start.4
  135.9 19.9 %collective-permute-start.5 = (bf16[256,256]{1,0:T(8,128)(2,1)}, bf16[256,256]{1,0:T(8,128)(2,1)}, u32[]{:S(2)}, u32[]{:S(2)}) collective-permute-start(bf16[256,256]{1,0:T(8,128)(2,1)} %copy.176), channel_id=1, source_target_pairs={{8,0},{12,4},{16,8},{20,12},{24,16},{28,20},{9,1},{13,5},{17,9},{2... | collective-permute-start | bytes 393224 | tf_op jit(solution)/shard_map/ppermute | solution.py:16
  145.5 10.4 %collective-permute-start.4 = (bf16[256,256]{1,0:T(8,128)(2,1)}, bf16[256,256]{1,0:T(8,128)(2,1)}, u32[]{:S(2)}, u32[]{:S(2)}) collective-permute-start(bf16[256,256]{1,0:T(8,128)(2,1)} %copy.174), channel_id=1, source_target_pairs={{4,0},{8,4},{12,8},{16,12},{20,16},{24,20},{28,24},{5,1},{9,5},{13... | collective-permute-start | bytes 393224 | tf_op jit(solution)/shard_map/ppermute | solution.py:16
Sparse Core Ops, SparseCore 0:
  10.1 80.4 all-gather.2
  92.2 23.8 all-gather.4
  119.2 30.9 reduce-scatter.1
where the time goes:
time: 167 us; the launch traced here: 165 us
  waiting for transfers between devices  75.8 us (45%)
  matrix products  32.5 us (19%)
  between operations  17.4 us (10%)
  starting transfers between devices  13.9 us (8%)
  local copies, waits for them, and re-layouts  13.7 us (8%)
  other arithmetic  11.3 us (7%)
    all_gather x1, waiting for transfers between devices, per_device(): lax.all_gather(out_weight, 'ctx', axis=0, tiled=True)  50.3 us
    all_gather x1, waiting for transfers between devices, per_device(): full_grad = lax.all_gather(out_grad, 'head', axis=1, tiled=True)  20.6 us
    ppermute x8, starting transfers between devices, shifted(): lax.ppermute(value, axis, [(source, source + steps) for source in range(l...  13.8 us
    dot_general x8, matrix products, masked_scores(): jnp.einsum('tgqd,cgd->gqtc', rows, key_block, preferred_element_type=jnp....  7.67 us
    cond x5, local copies, waits for them, and re-layouts, guarded(): lax.cond(flag, lambda unused: compute(), lambda unused: empty_fn(), 0)  5.69 us
    dot_general x4, matrix products, pair_grads(): jnp.einsum('gqtc,cgd->tgqd', grad_scores, key_block, preferred_element_ty...  5.55 us
    dot_general x1, matrix products, per_device(): jnp.einsum('tk,ck->tc', attended, lax.all_gather(out_weight, 'ctx', axis=...  4.83 us
    dot_general x4, matrix products, pair_grads(): jnp.einsum('tgqd,cgd->gqtc', grad_block, value_block, preferred_element_t...  4.48 us
  transfers between devices with their start and end apart: 11, of which 3 were waited for; matrix products, arithmetic and copies ran while one was open for 35% of the time, Pallas kernels for 0%

commit v1 on v0

v1 whole, which is shorter than its diff:
```python
import functools

import jax
import jax.numpy as jnp
from jax import lax
from jax.experimental import pallas as pl
from jax.experimental.pallas import tpu as pltpu
from jax.sharding import PartitionSpec as P

HEAD_DIM = 128
REACH = 4
NEGATIVE = -1e30
MESH = pl.DeviceIdType.MESH
F32 = jnp.float32
BF16 = jnp.bfloat16


def dot_nn(left, right):
    return jnp.dot(left, right, preferred_element_type=F32)


def dot_nt(left, right):
    return lax.dot_general(left, right, (((1,), (1,)), ((), ())), preferred_element_type=F32)


def loop(first, last, body, carried):
    if last - first > 8:
        return lax.fori_loop(first, last, body, carried)
    for index in range(first, last):
        carried = body(index, carried)
    return carried


def flip(value):
    return value.astype(F32).T.astype(BF16)


def kernel(
    n_ctx, n_head, pieces,
    doc_ref, q_ref, k_ref, v_ref, w_ref, g_ref,
    proj_ref, qg_ref, kg_ref, vg_ref,
    kv, kv_t, q_st, probs, probs_b, att, att_t, w_all, g_all, d_acc, d_st, d_t,
    delta, ds_b, dq_t, term, term_in, kv_out, kv_in, kv_acc,
    kv_send, kv_recv, w_send, w_recv, w_own, g_send, g_recv, g_own, t_send, t_recv, b_send, b_recv,
):
    rows = q_ref.shape[0]
    heads = q_ref.shape[1] // HEAD_DIM
    w_rows = w_ref.shape[0]
    cols = g_ref.shape[1]
    chain = n_ctx // 2
    scale = HEAD_DIM ** (-0.5)
    rank = lax.axis_index("ctx")
    mine = lax.axis_index("head")
    place = rank // 2
    side = rank % 2
    other = 1 - side
    core = mine % 2
    half = mine // 2
    mate = half * 2 + (1 - core)
    across = (1 - half) * 2 + core
    diagonal = (1 - half) * 2 + (1 - core)

    barrier = pltpu.get_barrier_semaphore()
    for target in (mate, across, diagonal):
        pl.semaphore_signal(barrier, inc=1, device_id=(rank, target), device_id_type=MESH)
    for step in range(1, REACH + 1):

        @pl.when(rank - step >= 0)
        def _(step=step):
            pl.semaphore_signal(barrier, inc=1, device_id=(rank - step, mine), device_id_type=MESH)

        @pl.when(rank + step < n_ctx)
        def _(step=step):
            pl.semaphore_signal(barrier, inc=1, device_id=(rank + step, mine), device_id_type=MESH)

    below_me = jnp.where(rank < REACH, rank, REACH)
    above_me = jnp.where(n_ctx - 1 - rank < REACH, n_ctx - 1 - rank, REACH)
    pl.semaphore_wait(barrier, n_head - 1 + below_me + above_me)

    def kv_copy(step, which):
        return pltpu.make_async_remote_copy(
            src_ref=(k_ref, v_ref)[which],
            dst_ref=kv.at[which, step],
            send_sem=kv_send.at[which, step],
            recv_sem=kv_recv.at[which, step],
            device_id=(rank + step, mine),
            device_id_type=MESH,
        )

    def w_slot(chunk, piece):
        first, count = pieces[piece]
        return w_all.at[pl.ds(pl.multiple_of(chunk * w_rows + first, 16), count), :]

    def w_copy(way, chunk, piece, own=False):
        first, count = pieces[piece]
        target = (rank + 2, rank - 2, place * 2 + other)[way]
        return pltpu.make_async_remote_copy(
            src_ref=w_ref.at[pl.ds(first, count), :] if own else w_slot(chunk, piece),
            dst_ref=w_slot(chunk, piece),
            send_sem=w_send.at[way, piece, chunk],
            recv_sem=w_recv.at[piece, chunk],
            device_id=(target, mine),
            device_id_type=MESH,
        )

    def g_copy(way):
        source, target = ((mine, mate), (mine, across), (across, mate))[way]
        return pltpu.make_async_remote_copy(
            src_ref=g_all.at[source] if way == 2 else g_ref,
            dst_ref=g_all.at[source],
            send_sem=g_send.at[way],
            recv_sem=g_recv.at[source],
            device_id=(rank, target),
            device_id_type=MESH,
        )

    def g_arrival(source):
        return pltpu.make_async_remote_copy(
            src_ref=g_ref,
            dst_ref=g_all.at[source],
            send_sem=g_send.at[0],
            recv_sem=g_recv.at[source],
            device_id=(rank, mate),
            device_id_type=MESH,
        )

    def term_copy(target):
        return pltpu.make_async_remote_copy(
            src_ref=term.at[target],
            dst_ref=term_in.at[mine],
            send_sem=t_send.at[target],
            recv_sem=t_recv.at[mine],
            device_id=(rank, target),
            device_id_type=MESH,
        )

    def term_arrival(source):
        return pltpu.make_async_remote_copy(
            src_ref=term.at[source],
            dst_ref=term_in.at[source],
            send_sem=t_send.at[source],
            recv_sem=t_recv.at[source],
            device_id=(rank, mate),
            device_id_type=MESH,
        )

    def back_copy(step):
        return pltpu.make_async_remote_copy(
            src_ref=kv_out.at[step],
            dst_ref=kv_in.at[step],
            send_sem=b_send.at[step],
            recv_sem=b_recv.at[step],
            device_id=(rank - step, mine),
            device_id_type=MESH,
        )

    piece_ids = range(len(pieces))

    def own_sends(act):
        for piece in piece_ids:

            @pl.when(place + 1 < chain)
            def _(piece=piece):
                act(w_copy(0, rank, piece, own=True))

            @pl.when(place >= 1)
            def _(piece=piece):
                act(w_copy(1, rank, piece, own=True))

            act(w_copy(2, rank, piece, own=True))

    for step in range(1, REACH + 1):

        @pl.when(rank + step < n_ctx)
        def _(step=step):
            kv_copy(step, 0).start()
            kv_copy(step, 1).start()

    own_sends(lambda copy: copy.start())
    g_copy(1).start()
    g_copy(0).start()
    own_rows = w_all.at[pl.ds(pl.multiple_of(rank * w_rows, 16), w_rows), :]
    w_local = pltpu.make_async_copy(w_ref, own_rows, w_own)
    w_local.start()
    g_local = pltpu.make_async_copy(g_ref, g_all.at[mine], g_own)
    g_local.start()

    lanes = [pl.ds(head * rows, rows) for head in range(heads)]
    for head in range(heads):
        q_st[lanes[head], :] = q_ref[:, head * HEAD_DIM:(head + 1) * HEAD_DIM]
    kv[0, 0] = k_ref[...]
    kv[1, 0] = v_ref[...]

    positions = rank * rows + lax.broadcasted_iota(jnp.int32, (1, rows), 1)

    def add_doc(index, carried):
        end, starts = carried
        length = doc_ref[index]
        end = end + length
        return end, starts + jnp.where(end <= positions, length, 0)

    _, starts = loop(
        0, doc_ref.shape[0], add_doc, (jnp.int32(0), jnp.zeros((1, rows), jnp.int32))
    )

    def score_block(step, maxima):
        @pl.when(jnp.logical_and(step > 0, rank - step >= 0))
        def _():
            for which in range(2):
                pltpu.make_async_remote_copy(
                    src_ref=(k_ref, v_ref)[which],
                    dst_ref=kv.at[which, step],
                    send_sem=kv_send.at[which, step],
                    recv_sem=kv_recv.at[which, step],
                    device_id=(rank, mate),
                    device_id_type=MESH,
                ).wait_recv()

        @pl.when(rank - step < 0)
        def _():
            kv[0, step] = jnp.zeros((rows, HEAD_DIM), BF16)
            kv[1, step] = jnp.zeros((rows, HEAD_DIM), BF16)

        key_block = kv[0, step]
        kv_t[0, step] = flip(key_block)
        kv_t[1, step] = flip(kv[1, step])
        key_pos = (rank - step) * rows + lax.broadcasted_iota(jnp.int32, (rows, rows), 0)
        allowed = jnp.logical_and(key_pos >= starts, key_pos <= positions)
        result = []
        for head in range(heads):
            scores = dot_nt(key_block, q_st[lanes[head], :]) * scale
            scores = jnp.where(allowed, scores, NEGATIVE)
            probs[step, :, lanes[head]] = scores
            result.append(jnp.maximum(maxima[head], jnp.max(scores, axis=0, keepdims=True)))
        return tuple(result)

    low = jnp.full((1, rows), NEGATIVE, F32)
    maxima = loop(0, REACH + 1, score_block, (low,) * heads)

    def exp_block(step, sums):
        result = []
        for head in range(heads):
            powers = jnp.exp(probs[step, :, lanes[head]] - maxima[head])
            probs[step, :, lanes[head]] = powers
            result.append(sums[head] + jnp.sum(powers, axis=0, keepdims=True))
        return tuple(result)

    zero = jnp.zeros((1, rows), F32)
    sums = loop(0, REACH + 1, exp_block, (zero,) * heads)
    inverses = [1.0 / total for total in sums]
    dq_t[...] = jnp.zeros_like(dq_t)

    def mix_block(step, carried):
        for head in range(heads):
            exact = probs[step, :, lanes[head]] * inverses[head]
            probs[step, :, lanes[head]] = exact
            probs_b[step, :, lanes[head]] = exact.astype(BF16)
        dq_t[...] += dot_nn(kv_t[1, step], probs_b[step])
        return carried

    loop(0, REACH + 1, mix_block, 0)
    for head in range(heads):
        mixed = dq_t[:, lanes[head]]
        att_t[:, lanes[head]] = mixed.astype(BF16)
        att[:, head * HEAD_DIM:(head + 1) * HEAD_DIM] = mixed.T.astype(BF16)

    w_local.wait()
    g_local.wait()
    g_arrival(across).wait_recv()
    g_copy(2).start()
    g_arrival(mate).wait_recv()
    g_arrival(diagonal).wait_recv()
    d_acc[...] = jnp.zeros_like(d_acc)

    def process(block):
        w_block = w_all[pl.ds(pl.multiple_of(block * cols, cols), cols), :]
        d_acc[...] += dot_nn(g_all[block], w_block)
        term[block] = dot_nt(att[...], w_block).astype(BF16)

        @pl.when(block != mine)
        def _():
            term_copy(block).start()

    def x_wait(chunk):
        for piece in piece_ids:
            w_copy(2, chunk, piece).wait_recv()

    early = 2 * w_rows == cols

    def finish(step):
        def one(which, carried):
            spot = place + (2 * which - 1) * step

            @pl.when(jnp.logical_and(spot >= 0, spot < chain) & (which + step > 0))
            def _():
                x_wait(spot * 2 + other)
                if early:
                    process(spot)

            return carried

        loop(0, 2, one, 0)

    def hop(step, carried):
        below = place - step
        above = place + step
        for piece in piece_ids:

            @pl.when(below >= 0)
            def _(piece=piece):
                chunk = below * 2 + side
                w_copy(0, chunk, piece).wait_recv()

                @pl.when(place + 1 < chain)
                def _():
                    w_copy(0, chunk, piece).start()

                w_copy(2, chunk, piece).start()

            @pl.when(above < chain)
            def _(piece=piece):
                chunk = above * 2 + side
                w_copy(1, chunk, piece).wait_recv()

                @pl.when(place >= 1)
                def _():
                    w_copy(1, chunk, piece).start()

                w_copy(2, chunk, piece).start()

        finish(step - 1)
        return carried

    loop(1, chain, hop, 0)
    finish(chain - 1)
    if not early:

        def late(block, carried):
            process(block)
            return carried

        loop(0, n_head, late, 0)

    for head in range(heads):
        part = d_acc[:, head * HEAD_DIM:(head + 1) * HEAD_DIM].astype(BF16)
        d_st[lanes[head], :] = part
        turned = part.astype(F32).T
        delta[:, lanes[head]] = jnp.sum(
            turned * att_t[:, lanes[head]].astype(F32), axis=0, keepdims=True
        )
    dq_t[...] = jnp.zeros_like(dq_t)

    def grad_block(index, carried):
        step = REACH - index
        value_block = kv[1, step]
        for head in range(heads):
            d_probs = dot_nt(value_block, d_st[lanes[head], :])
            d_scores = probs[step, :, lanes[head]] * (d_probs - delta[:, lanes[head]])
            ds_b[:, lanes[head]] = d_scores.astype(BF16)
        key_part = dot_nn(ds_b[...], q_st[...])
        value_part = dot_nn(probs_b[step], d_st[...])

        @pl.when(step == 0)
        def _():
            kv_acc[0] = key_part
            kv_acc[1] = value_part

        @pl.when(jnp.logical_and(step > 0, rank - step >= 0))
        def _():
            kv_out[step, 0] = key_part.astype(BF16)
            kv_out[step, 1] = value_part.astype(BF16)
            back_copy(step).start()

        dq_t[...] += dot_nn(kv_t[0, step], ds_b[...])
        return carried

    loop(0, REACH + 1, grad_block, 0)
    for head in range(heads):
        qg_ref[:, head * HEAD_DIM:(head + 1) * HEAD_DIM] = (
            (dq_t[:, lanes[head]] * scale).T.astype(BF16)
        )

    for source in (mate, across, diagonal):
        term_arrival(source).wait_recv()
    summed = term[mine].astype(F32)
    for source in (mate, across, diagonal):
        summed = summed + term_in[source].astype(F32)
    proj_ref[...] = summed.astype(BF16)

    for step in range(REACH, 0, -1):

        @pl.when(rank + step < n_ctx)
        def _(step=step):
            back_copy(step).wait_recv()
            kv_acc[...] += kv_in[step].astype(F32)

    kg_ref[...] = (kv_acc[0] * scale).astype(BF16)
    vg_ref[...] = kv_acc[1].astype(BF16)

    for step in range(1, REACH + 1):

        @pl.when(rank + step < n_ctx)
        def _(step=step):
            kv_copy(step, 0).wait_send()
            kv_copy(step, 1).wait_send()

        @pl.when(rank - step >= 0)
        def _(step=step):
            back_copy(step).wait_send()

    own_sends(lambda copy: copy.wait_send())

    def drain(step, carried):
        below = place - step
        above = place + step
        for piece in piece_ids:

            @pl.when(below >= 0)
            def _(piece=piece):
                chunk = below * 2 + side

                @pl.when(place + 1 < chain)
                def _():
                    w_copy(0, chunk, piece).wait_send()

                w_copy(2, chunk, piece).wait_send()

            @pl.when(above < chain)
            def _(piece=piece):
                chunk = above * 2 + side

                @pl.when(place >= 1)
                def _():
                    w_copy(1, chunk, piece).wait_send()

                w_copy(2, chunk, piece).wait_send()

        return carried

    loop(1, chain, drain, 0)
    for way in range(3):
        g_copy(way).wait_send()
    for target in (mate, across, diagonal):
        term_copy(target).wait_send()


def per_device(n_ctx, n_head, queries, key_states, value_states, doc_lengths, out_weight, out_grad):
    rows, q_cols = queries.shape
    heads = q_cols // HEAD_DIM
    wide = heads * rows
    w_rows = out_weight.shape[0]
    cols = out_grad.shape[1]
    blocks = REACH + 1
    pieces = ((0, w_rows // 2), (w_rows // 2, w_rows // 2))
    vmem = pl.BlockSpec(memory_space=pltpu.VMEM)
    hbm = pl.BlockSpec(memory_space=pl.ANY)
    dma = pltpu.SemaphoreType.DMA
    count = len(pieces)
    return pl.pallas_call(
        functools.partial(kernel, n_ctx, n_head, pieces),
        out_shape=(
            jax.ShapeDtypeStruct(out_grad.shape, BF16),
            jax.ShapeDtypeStruct(queries.shape, BF16),
            jax.ShapeDtypeStruct(key_states.shape, BF16),
            jax.ShapeDtypeStruct(value_states.shape, BF16),
        ),
        in_specs=[pl.BlockSpec(memory_space=pltpu.SMEM), vmem, vmem, vmem, hbm, hbm],
        out_specs=(vmem,) * 4,
        scratch_shapes=[
            pltpu.VMEM((2, blocks, rows, HEAD_DIM), BF16),
            pltpu.VMEM((2, blocks, HEAD_DIM, rows), BF16),
            pltpu.VMEM((wide, HEAD_DIM), BF16),
            pltpu.VMEM((blocks, rows, wide), F32),
            pltpu.VMEM((blocks, rows, wide), BF16),
            pltpu.VMEM((rows, q_cols), BF16),
            pltpu.VMEM((HEAD_DIM, wide), BF16),
            pltpu.VMEM((n_ctx * w_rows, q_cols), BF16),
            pltpu.VMEM((n_head, rows, cols), BF16),
            pltpu.VMEM((rows, q_cols), F32),
            pltpu.VMEM((wide, HEAD_DIM), BF16),
            pltpu.VMEM((HEAD_DIM, wide), BF16),
            pltpu.VMEM((1, wide), F32),
            pltpu.VMEM((rows, wide), BF16),
            pltpu.VMEM((HEAD_DIM, wide), F32),
            pltpu.VMEM((n_head, rows, cols), BF16),
            pltpu.VMEM((n_head, rows, cols), BF16),
            pltpu.VMEM((blocks, 2, rows, HEAD_DIM), BF16),
            pltpu.VMEM((blocks, 2, rows, HEAD_DIM), BF16),
            pltpu.VMEM((2, rows, HEAD_DIM), F32),
            dma((2, blocks)),
            dma((2, blocks)),
            dma((3, count, n_ctx)),
            dma((count, n_ctx)),
            dma,
            dma((3,)),
            dma((n_head,)),
            dma,
            dma((n_head,)),
            dma((n_head,)),
            dma((blocks,)),
            dma((blocks,)),
        ],
        compiler_params=pltpu.CompilerParams(
            collective_id=0, has_side_effects=True, vmem_limit_bytes=48 * 1024 * 1024
        ),
    )(doc_lengths, queries, key_states, value_states, out_weight, out_grad)


def solution(mesh):
    whole = P("ctx", "head")
    return jax.shard_map(
        functools.partial(per_device, mesh.shape["ctx"], mesh.shape["head"]),
        mesh=mesh,
        in_specs=(whole, whole, whole, P(), whole, whole),
        out_specs=(whole,) * 4,
        check_vma=False,
    )
```

time: 167 us -> 89.9 us (0.54)
  the two profiles are of different devices: /device:TPU:27 before, /device:TPU:14 now
where the time goes in v1:
time: 89.9 us; the launch traced here: 89.5 us
  Pallas kernels  80.8 us (90%)
  local copies, waits for them, and re-layouts  8.11 us (9%)
    pallas_call x1, Pallas kernels, per_device(): pl.pallas_call(functools.partial(kernel, n_ctx, n_head, pieces), out_shap...  80.8 us
    unnamed x16, local copies, waits for them, and re-layouts  8.11 us

profile of v1, /device:TPU:14, one launch (start us, length us, event | category | flops | bytes accessed | tf_op | source)
XLA Modules:
  0.0 89.5 jit_solution(14123360270261873171)
XLA Ops:
  0.6 0.0 copy-start
  0.6 1.0 %copy-done = bf16[512,512]{1,0:T(8,128)(2,1)S(1)} copy-done((bf16[512,512]{1,0:T(8,128)(2,1)S(1)}, bf16[512,512]{1,0:T(8,128)(2,1)}, u32[]{:S(2)}) %copy-start) | copy-done | bytes 524312
  1.7 0.0 copy-start.1
  1.7 1.0 %copy-done.1 = bf16[256,1024]{1,0:T(8,128)(2,1)S(1)} copy-done((bf16[256,1024]{1,0:T(8,128)(2,1)S(1)}, bf16[256,1024]{1,0:T(8,128)(2,1)}, u32[]{:S(2)}) %copy-start.1) | copy-done | bytes 524312
  2.7 0.0 copy-start.2
  2.7 0.9 %copy-done.2 = bf16[256,512]{1,0:T(8,128)(2,1)S(1)} copy-done((bf16[256,512]{1,0:T(8,128)(2,1)S(1)}, bf16[256,512]{1,0:T(8,128)(2,1)}, u32[]{:S(2)}) %copy-start.2) | copy-done | bytes 262168
  3.7 0.0 copy-start.3
  3.7 0.8 copy-done.3
  4.5 0.0 copy-start.4
  4.5 0.8 copy-done.4
  5.3 0.0 copy-start.5
  5.3 0.7 copy-done.5
  6.0 80.8 %shard_map.93 = (bf16[256,1024]{1,0:T(8,128)(2,1)S(1)}, bf16[256,512]{1,0:T(8,128)(2,1)S(1)}, bf16[256,128]{1,0:T(8,128)(2,1)S(1)}, bf16[256,128]{1,0:T(8,128)(2,1)S(1)}) custom-call(s32[4]{0:T(128)S(1)} %copy-done.5, bf16[256,512]{1,0:T(8,128)(2,1)S(1)} %copy-done.2, bf16[256,128]{1,0:T(8,128)(2,1)S(1)} %copy-done.3, bf16[256,128]{1,0:T(8,128)(2,1)S(1)} %copy-done.4, ...), custom_call_target="tpu_custom_call" | custom-call | tf_op jit(solution)/shard_map/pallas_call | solution.py:459
  86.8 0.8 copy.14
  87.6 0.7 copy.15
  88.3 0.6 copy.16
  88.9 0.6 copy.17
Async XLA Ops:
  0.6 1.0 %copy-start = (bf16[512,512]{1,0:T(8,128)(2,1)S(1)}, bf16[512,512]{1,0:T(8,128)(2,1)}, u32[]{:S(2)}) copy-start(bf16[512,512]{1,0:T(8,128)(2,1)} %w_ref.1) | copy-start | bytes 1572868
  1.7 1.0 %copy-start.1 = (bf16[256,1024]{1,0:T(8,128)(2,1)S(1)}, bf16[256,1024]{1,0:T(8,128)(2,1)}, u32[]{:S(2)}) copy-start(bf16[256,1024]{1,0:T(8,128)(2,1)} %g_ref.1) | copy-start | bytes 1572868
  2.7 0.9 %copy-start.2 = (bf16[256,512]{1,0:T(8,128)(2,1)S(1)}, bf16[256,512]{1,0:T(8,128)(2,1)}, u32[]{:S(2)}) copy-start(bf16[256,512]{1,0:T(8,128)(2,1)} %q_ref.1) | copy-start | bytes 786436
  3.7 0.8 copy-start.3
  4.5 0.8 copy-start.4
  5.3 0.7 copy-start.5

commit v2 on v1

--- a/solution.py
+++ b/solution.py
@@ -9,6 +9,7 @@
 
 HEAD_DIM = 128
 REACH = 4
+TILE = 256
 NEGATIVE = -1e30
 MESH = pl.DeviceIdType.MESH
 F32 = jnp.float32
@@ -39,7 +40,7 @@
     n_ctx, n_head, pieces,
     doc_ref, q_ref, k_ref, v_ref, w_ref, g_ref,
     proj_ref, qg_ref, kg_ref, vg_ref,
-    kv, kv_t, q_st, probs, probs_b, att, att_t, w_all, g_all, d_acc, d_st, d_t,
+    kv, kv_t, q_st, probs, probs_b, att, att_t, w_all, g_all, d_acc, d_st,
     delta, ds_b, dq_t, term, term_in, kv_out, kv_in, kv_acc,
     kv_send, kv_recv, w_send, w_recv, w_own, g_send, g_recv, g_own, t_send, t_recv, b_send, b_recv,
 ):
@@ -48,6 +49,7 @@
     w_rows = w_ref.shape[0]
     cols = g_ref.shape[1]
     chain = n_ctx // 2
+    tiles, tile = term_in.shape[1], term_in.shape[3]
     scale = HEAD_DIM ** (-0.5)
     rank = lax.axis_index("ctx")
     mine = lax.axis_index("head")
@@ -124,22 +126,22 @@
             device_id_type=MESH,
         )
 
-    def term_copy(target):
-        return pltpu.make_async_remote_copy(
-            src_ref=term.at[target],
-            dst_ref=term_in.at[mine],
-            send_sem=t_send.at[target],
-            recv_sem=t_recv.at[mine],
-            device_id=(rank, target),
-            device_id_type=MESH,
-        )
-
-    def term_arrival(source):
-        return pltpu.make_async_remote_copy(
-            src_ref=term.at[source],
-            dst_ref=term_in.at[source],
-            send_sem=t_send.at[source],
-            recv_sem=t_recv.at[source],
+    def term_copy(index):
+        return pltpu.make_async_remote_copy(
+            src_ref=term.at[index],
+            dst_ref=term_in.at[mine, index % tiles],
+            send_sem=t_send.at[index],
+            recv_sem=t_recv.at[mine, index % tiles],
+            device_id=(rank, index // tiles),
+            device_id_type=MESH,
+        )
+
+    def term_arrival(source, index):
+        return pltpu.make_async_remote_copy(
+            src_ref=term.at[index],
+            dst_ref=term_in.at[source, index],
+            send_sem=t_send.at[index],
+            recv_sem=t_recv.at[source, index],
             device_id=(rank, mate),
             device_id_type=MESH,
         )
@@ -250,6 +252,35 @@
     inverses = [1.0 / total for total in sums]
     dq_t[...] = jnp.zeros_like(dq_t)
 
+    def relays(step):
+        below = place - step
+        above = place + step
+        for piece in piece_ids:
+
+            @pl.when(below >= 0)
+            def _(piece=piece):
+                chunk = below * 2 + side
+                w_copy(0, chunk, piece).wait_recv()
+
+                @pl.when(place + 1 < chain)
+                def _():
+                    w_copy(0, chunk, piece).start()
+
+                w_copy(2, chunk, piece).start()
+
+            @pl.when(above < chain)
+            def _(piece=piece):
+                chunk = above * 2 + side
+                w_copy(1, chunk, piece).wait_recv()
+
+                @pl.when(place >= 1)
+                def _():
+                    w_copy(1, chunk, piece).start()
+
+                w_copy(2, chunk, piece).start()
+
+    relays(1)
+
     def mix_block(step, carried):
         for head in range(heads):
             exact = probs[step, :, lanes[head]] * inverses[head]
@@ -272,74 +303,59 @@
     g_arrival(diagonal).wait_recv()
     d_acc[...] = jnp.zeros_like(d_acc)
 
-    def process(block):
-        w_block = w_all[pl.ds(pl.multiple_of(block * cols, cols), cols), :]
-        d_acc[...] += dot_nn(g_all[block], w_block)
-        term[block] = dot_nt(att[...], w_block).astype(BF16)
-
-        @pl.when(block != mine)
+    def process(index):
+        w_tile = w_all[pl.ds(pl.multiple_of(index * tile, tile), tile), :]
+        first = pl.multiple_of(index % tiles * tile, tile)
+        d_acc[...] += dot_nn(g_all[index // tiles, :, pl.ds(first, tile)], w_tile)
+        term[index] = dot_nt(att[...], w_tile).astype(BF16)
+
+        @pl.when(index // tiles != mine)
         def _():
-            term_copy(block).start()
-
-    def x_wait(chunk):
+            term_copy(index).start()
+
+    early = w_rows == len(pieces) * tile
+
+    def count_of(step):
+        return 1 if isinstance(step, int) and step == 0 else 2
+
+    def finish(step):
         for piece in piece_ids:
-            w_copy(2, chunk, piece).wait_recv()
-
-    early = 2 * w_rows == cols
-
-    def finish(step):
-        def one(which, carried):
-            spot = place + (2 * which - 1) * step
-
-            @pl.when(jnp.logical_and(spot >= 0, spot < chain) & (which + step > 0))
-            def _():
-                x_wait(spot * 2 + other)
-                if early:
-                    process(spot)
-
-            return carried
-
-        loop(0, 2, one, 0)
-
-    def hop(step, carried):
-        below = place - step
-        above = place + step
-        for piece in piece_ids:
-
-            @pl.when(below >= 0)
-            def _(piece=piece):
-                chunk = below * 2 + side
-                w_copy(0, chunk, piece).wait_recv()
-
-                @pl.when(place + 1 < chain)
-                def _():
-                    w_copy(0, chunk, piece).start()
-
-                w_copy(2, chunk, piece).start()
-
-            @pl.when(above < chain)
-            def _(piece=piece):
-                chunk = above * 2 + side
-                w_copy(1, chunk, piece).wait_recv()
-
-                @pl.when(place >= 1)
-                def _():
-                    w_copy(1, chunk, piece).start()
-
-                w_copy(2, chunk, piece).start()
-
+            for spot in (place - step, place + step)[:count_of(step)]:
+
+                @pl.when(jnp.logical_and(spot >= 0, spot < chain))
+                def _(piece=piece, spot=spot):
+                    chunk = spot * 2 + other
+                    w_copy(2, chunk, piece).wait_recv()
+                    if early:
+                        process(chunk * len(pieces) + piece)
+
+    def direct(step):
+        if early:
+            for piece in piece_ids:
+                for spot in (place - step, place + step)[:count_of(step)]:
+
+                    @pl.when(jnp.logical_and(spot >= 0, spot < chain))
+                    def _(piece=piece, spot=spot):
+                        process((spot * 2 + side) * len(pieces) + piece)
+
+    def later(step, carried):
+        relays(step)
         finish(step - 1)
+        direct(step)
         return carried
 
-    loop(1, chain, hop, 0)
+    direct(0)
+    finish(0)
+    direct(1)
+    loop(2, chain, later, 0)
     finish(chain - 1)
     if not early:
 
-        def late(block, carried):
-            process(block)
+        def late(index, carried):
+            process(index)
             return carried
 
-        loop(0, n_head, late, 0)
+        loop(0, n_head * tiles, late, 0)
 
     for head in range(heads):
         part = d_acc[:, head * HEAD_DIM:(head + 1) * HEAD_DIM].astype(BF16)
@@ -380,12 +396,12 @@
             (dq_t[:, lanes[head]] * scale).T.astype(BF16)
         )
 
-    for source in (mate, across, diagonal):
-        term_arrival(source).wait_recv()
-    summed = term[mine].astype(F32)
-    for source in (mate, across, diagonal):
-        summed = summed + term_in[source].astype(F32)
-    proj_ref[...] = summed.astype(BF16)
+    for index in range(tiles):
+        summed = term[mine * tiles + index].astype(F32)
+        for source in (mate, across, diagonal):
+            term_arrival(source, index).wait_recv()
+            summed = summed + term_in[source, index].astype(F32)
+        proj_ref[:, index * tile:(index + 1) * tile] = summed.astype(BF16)
 
     for step in range(REACH, 0, -1):
 
@@ -440,8 +456,11 @@
     loop(1, chain, drain, 0)
     for way in range(3):
         g_copy(way).wait_send()
-    for target in (mate, across, diagonal):
-        term_copy(target).wait_send()
+    for index in range(n_head * tiles):
+
+        @pl.when(mine != index // tiles)
+        def _(index=index):
+            term_copy(index).wait_send()
 
 
 def per_device(n_ctx, n_head, queries, key_states, value_states, doc_lengths, out_weight, out_grad):
@@ -451,6 +470,8 @@
     w_rows = out_weight.shape[0]
     cols = out_grad.shape[1]
     blocks = REACH + 1
+    tile = min(TILE, cols)
+    tiles = cols // tile
     pieces = ((0, w_rows // 2), (w_rows // 2, w_rows // 2))
     vmem = pl.BlockSpec(memory_space=pltpu.VMEM)
     hbm = pl.BlockSpec(memory_space=pl.ANY)
@@ -478,12 +499,11 @@
             pltpu.VMEM((n_head, rows, cols), BF16),
             pltpu.VMEM((rows, q_cols), F32),
             pltpu.VMEM((wide, HEAD_DIM), BF16),
-            pltpu.VMEM((HEAD_DIM, wide), BF16),
             pltpu.VMEM((1, wide), F32),
             pltpu.VMEM((rows, wide), BF16),
             pltpu.VMEM((HEAD_DIM, wide), F32),
-            pltpu.VMEM((n_head, rows, cols), BF16),
-            pltpu.VMEM((n_head, rows, cols), BF16),
+            pltpu.VMEM((n_head * tiles, rows, tile), BF16),
+            pltpu.VMEM((n_head, tiles, rows, tile), BF16),
             pltpu.VMEM((blocks, 2, rows, HEAD_DIM), BF16),
             pltpu.VMEM((blocks, 2, rows, HEAD_DIM), BF16),
             pltpu.VMEM((2, rows, HEAD_DIM), F32),
@@ -495,13 +515,13 @@
             dma((3,)),
             dma((n_head,)),
             dma,
-            dma((n_head,)),
-            dma((n_head,)),
+            dma((n_head * tiles,)),
+            dma((n_head, tiles)),
             dma((blocks,)),
             dma((blocks,)),
         ],
         compiler_params=pltpu.CompilerParams(
-            collective_id=0, has_side_effects=True, vmem_limit_bytes=48 * 1024 * 1024
+            collective_id=0, has_side_effects=True, vmem_limit_bytes=60 * 1024 * 1024
         ),
     )(doc_lengths, queries, key_states, value_states, out_weight, out_grad)
 

time: 89.9 us -> 86.2 us (0.959)
  local copies, waits for them, and re-layouts: 8.11 us -> 4.27 us
    unnamed x16 -> x10, local copies, waits for them, and re-layouts: 8.11 us -> 4.27 us
where the time goes in v2:
time: 86.2 us; the launch traced here: 85.9 us
  Pallas kernels  81 us (94%)
  local copies, waits for them, and re-layouts  4.27 us (5%)
    pallas_call x1, Pallas kernels, per_device(): pl.pallas_call(functools.partial(kernel, n_ctx, n_head, pieces), out_shap...  81 us
    unnamed x10, local copies, waits for them, and re-layouts  4.27 us

profile of v2, /device:TPU:14, one launch (start us, length us, event | category | flops | bytes accessed | tf_op | source)
XLA Modules:
  0.0 85.9 jit_solution(12216795790489989204)
XLA Ops:
  0.6 81.0 %shard_map.93 = (bf16[256,1024]{1,0:T(8,128)(2,1)}, bf16[256,512]{1,0:T(8,128)(2,1)}, bf16[256,128]{1,0:T(8,128)(2,1)}, bf16[256,128]{1,0:T(8,128)(2,1)}) custom-call(s32[4]{0:T(128)} %doc_ref.1, bf16[256,512]{1,0:T(8,128)(2,1)} %q_ref.1, bf16[256,128]{1,0:T(8,128)(2,1)} %k_ref.1, bf16[256,128]{1,0:T(8,128)(2,1)} %v_ref.1, bf16[512,512]{1,0:T(8,128)(2,1)} %w_ref.1, ...), custom_call_target="tpu_custom_call" | custom-call | tf_op jit(solution)/shard_map/pallas_call | solution.py:480
  81.6 0.0 copy-start
  81.6 1.9 %copy.14 = bf16[256,1024]{1,0:T(8,128)(2,1)} copy(bf16[256,1024]{1,0:T(8,128)(2,1)} %get-tuple-element.8) | data formatting | bytes 1048576
  83.6 0.0 copy-done
  83.6 0.0 copy-start.2
  83.6 0.7 copy.15
  84.3 0.2 copy-done.2
  84.4 0.0 copy-start.1
  84.4 0.6 copy.16
  85.0 0.2 copy-done.1
  85.3 0.6 copy.17
Async XLA Ops:
  81.6 1.9 %copy-start = (bf16[256,512]{1,0:T(8,128)(2,1)S(1)}, bf16[256,512]{1,0:T(8,128)(2,1)}, u32[]{:S(2)}) copy-start(bf16[256,512]{1,0:T(8,128)(2,1)} %get-tuple-element.9) | copy-start | bytes 786436
  83.6 0.9 %copy-start.2 = (bf16[256,128]{1,0:T(8,128)(2,1)S(1)}, bf16[256,128]{1,0:T(8,128)(2,1)}, u32[]{:S(2)}) copy-start(bf16[256,128]{1,0:T(8,128)(2,1)} %get-tuple-element.10) | copy-start | bytes 196612
  84.4 0.9 %copy-start.1 = (bf16[256,128]{1,0:T(8,128)(2,1)S(1)}, bf16[256,128]{1,0:T(8,128)(2,1)}, u32[]{:S(2)}) copy-start(bf16[256,128]{1,0:T(8,128)(2,1)} %get-tuple-element.11) | copy-start | bytes 196612

commit v3 on v2

--- a/solution.py
+++ b/solution.py
@@ -62,6 +62,8 @@
     across = (1 - half) * 2 + core
     diagonal = (1 - half) * 2 + (1 - core)
 
+    kv[0, 0] = k_ref[...]
+    kv[0, 1] = v_ref[...]
     barrier = pltpu.get_barrier_semaphore()
     for target in (mate, across, diagonal):
         pl.semaphore_signal(barrier, inc=1, device_id=(rank, target), device_id_type=MESH)
@@ -79,15 +81,46 @@
     above_me = jnp.where(n_ctx - 1 - rank < REACH, n_ctx - 1 - rank, REACH)
     pl.semaphore_wait(barrier, n_head - 1 + below_me + above_me)
 
-    def kv_copy(step, which):
-        return pltpu.make_async_remote_copy(
-            src_ref=(k_ref, v_ref)[which],
-            dst_ref=kv.at[which, step],
-            send_sem=kv_send.at[which, step],
-            recv_sem=kv_recv.at[which, step],
-            device_id=(rank + step, mine),
-            device_id_type=MESH,
-        )
+    def kv_copy(way):
+        source, slot, target = (
+            (0, 1 + REACH * side, place * 2 + other),
+            (0, 2, rank + 2),
+            (0, 4, rank + 4),
+            (1 + REACH * other, 1 + 2 * side, rank + 2),
+            (1 + REACH, 3, rank + 4),
+        )[way]
+        return pltpu.make_async_remote_copy(
+            src_ref=kv.at[source],
+            dst_ref=kv.at[slot],
+            send_sem=kv_send.at[way],
+            recv_sem=kv_recv.at[slot],
+            device_id=(target, mine),
+            device_id_type=MESH,
+        )
+
+    def kv_arrival(slot):
+        return pltpu.make_async_remote_copy(
+            src_ref=kv.at[0],
+            dst_ref=kv.at[slot],
+            send_sem=kv_send.at[0],
+            recv_sem=kv_recv.at[slot],
+            device_id=(rank, mate),
+            device_id_type=MESH,
+        )
+
+    def kv_sends(ways, act):
+        for way in ways:
+            needed = (
+                place >= 0,
+                place + 1 < chain,
+                place + 2 < chain,
+                place + 1 < chain,
+                jnp.logical_and(place + 2 < chain, side == 0),
+            )[way]
+
+            @pl.when(needed)
+            def _(way=way):
+                act(kv_copy(way))
 
     def w_slot(chunk, piece):
         first, count = pieces[piece]
@@ -158,27 +191,30 @@
 
     piece_ids = range(len(pieces))
 
+    def start(copy):
+        copy.start()
+
+    def wait_send(copy):
+        copy.wait_send()
+
     def own_sends(act):
+        for piece in piece_ids:
+
+            @pl.when(place >= 1)
+            def _(piece=piece):
+                act(w_copy(1, rank, piece, own=True))
+
+            act(w_copy(2, rank, piece, own=True))
+
+    def own_up(act):
         for piece in piece_ids:
 
             @pl.when(place + 1 < chain)
             def _(piece=piece):
                 act(w_copy(0, rank, piece, own=True))
 
-            @pl.when(place >= 1)
-            def _(piece=piece):
-                act(w_copy(1, rank, piece, own=True))
-
-            act(w_copy(2, rank, piece, own=True))
-
-    for step in range(1, REACH + 1):
-
-        @pl.when(rank + step < n_ctx)
-        def _(step=step):
-            kv_copy(step, 0).start()
-            kv_copy(step, 1).start()
-
-    own_sends(lambda copy: copy.start())
+    kv_sends(range(3), start)
+    own_sends(start)
     g_copy(1).start()
     g_copy(0).start()
     own_rows = w_all.at[pl.ds(pl.multiple_of(rank * w_rows, 16), w_rows), :]
@@ -187,11 +223,13 @@
     g_local = pltpu.make_async_copy(g_ref, g_all.at[mine], g_own)
     g_local.start()
 
+    kv_arrival(1 + REACH * other).wait_recv()
+    kv_sends(range(3, 5), start)
+    own_up(start)
+
     lanes = [pl.ds(head * rows, rows) for head in range(heads)]
     for head in range(heads):
         q_st[lanes[head], :] = q_ref[:, head * HEAD_DIM:(head + 1) * HEAD_DIM]
-    kv[0, 0] = k_ref[...]
-    kv[1, 0] = v_ref[...]
 
     positions = rank * rows + lax.broadcasted_iota(jnp.int32, (1, rows), 1)
 
@@ -206,26 +244,19 @@
     )
 
     def score_block(step, maxima):
-        @pl.when(jnp.logical_and(step > 0, rank - step >= 0))
-        def _():
-            for which in range(2):
-                pltpu.make_async_remote_copy(
-                    src_ref=(k_ref, v_ref)[which],
-                    dst_ref=kv.at[which, step],
-                    send_sem=kv_send.at[which, step],
-                    recv_sem=kv_recv.at[which, step],
-                    device_id=(rank, mate),
-                    device_id_type=MESH,
-                ).wait_recv()
+        if step > 0:
+
+            @pl.when(jnp.logical_and(rank - step >= 0, jnp.logical_or(step > 1, side == 0)))
+            def _():
+                kv_arrival(step).wait_recv()
 
         @pl.when(rank - step < 0)
         def _():
-            kv[0, step] = jnp.zeros((rows, HEAD_DIM), BF16)
-            kv[1, step] = jnp.zeros((rows, HEAD_DIM), BF16)
-
-        key_block = kv[0, step]
+            kv[step] = jnp.zeros((2, rows, HEAD_DIM), BF16)
+
+        key_block = kv[step, 0]
         kv_t[0, step] = flip(key_block)
-        kv_t[1, step] = flip(kv[1, step])
+        kv_t[1, step] = flip(kv[step, 1])
         key_pos = (rank - step) * rows + lax.broadcasted_iota(jnp.int32, (rows, rows), 0)
         allowed = jnp.logical_and(key_pos >= starts, key_pos <= positions)
         result = []
@@ -368,7 +399,7 @@
 
     def grad_block(index, carried):
         step = REACH - index
-        value_block = kv[1, step]
+        value_block = kv[step, 1]
         for head in range(heads):
             d_probs = dot_nt(value_block, d_st[lanes[head], :])
             d_scores = probs[step, :, lanes[head]] * (d_probs - delta[:, lanes[head]])
@@ -415,16 +446,13 @@
 
     for step in range(1, REACH + 1):
 
-        @pl.when(rank + step < n_ctx)
-        def _(step=step):
-            kv_copy(step, 0).wait_send()
-            kv_copy(step, 1).wait_send()
-
         @pl.when(rank - step >= 0)
         def _(step=step):
             back_copy(step).wait_send()
 
-    own_sends(lambda copy: copy.wait_send())
+    own_sends(wait_send)
+    own_up(wait_send)
+    kv_sends(range(5), wait_send)
 
     def drain(step, carried):
         below = place - step
@@ -488,7 +516,7 @@
         in_specs=[pl.BlockSpec(memory_space=pltpu.SMEM), vmem, vmem, vmem, hbm, hbm],
         out_specs=(vmem,) * 4,
         scratch_shapes=[
-            pltpu.VMEM((2, blocks, rows, HEAD_DIM), BF16),
+            pltpu.VMEM((blocks + 1, 2, rows, HEAD_DIM), BF16),
             pltpu.VMEM((2, blocks, HEAD_DIM, rows), BF16),
             pltpu.VMEM((wide, HEAD_DIM), BF16),
             pltpu.VMEM((blocks, rows, wide), F32),
@@ -507,8 +535,8 @@
             pltpu.VMEM((blocks, 2, rows, HEAD_DIM), BF16),
             pltpu.VMEM((blocks, 2, rows, HEAD_DIM), BF16),
             pltpu.VMEM((2, rows, HEAD_DIM), F32),
-            dma((2, blocks)),
-            dma((2, blocks)),
+            dma((blocks,)),
+            dma((blocks + 1,)),
             dma((3, count, n_ctx)),
             dma((count, n_ctx)),
             dma,

time: 86.2 us -> 81.3 us (0.943)
  Pallas kernels: 81 us -> 76.1 us
    pallas_call x1, Pallas kernels: 81 us -> 76.1 us  [per_device(): pl.pallas_call(functools.partial(kernel, n_ctx, n_head, pieces), out_shap...]
where the time goes in v3:
time: 81.3 us; the launch traced here: 81 us
  Pallas kernels  76.1 us (94%)
  local copies, waits for them, and re-layouts  4.27 us (5%)
    pallas_call x1, Pallas kernels, per_device(): pl.pallas_call(functools.partial(kernel, n_ctx, n_head, pieces), out_shap...  76.1 us
    unnamed x10, local copies, waits for them, and re-layouts  4.27 us

profile of v3, /device:TPU:14, one launch (start us, length us, event | category | flops | bytes accessed | tf_op | source)
XLA Modules:
  0.0 81.0 jit_solution(7439236417103980746)
XLA Ops:
  0.6 76.1 %shard_map.93 = (bf16[256,1024]{1,0:T(8,128)(2,1)}, bf16[256,512]{1,0:T(8,128)(2,1)}, bf16[256,128]{1,0:T(8,128)(2,1)}, bf16[256,128]{1,0:T(8,128)(2,1)}) custom-call(s32[4]{0:T(128)} %doc_ref.1, bf16[256,512]{1,0:T(8,128)(2,1)} %q_ref.1, bf16[256,128]{1,0:T(8,128)(2,1)} %k_ref.1, bf16[256,128]{1,0:T(8,128)(2,1)} %v_ref.1, bf16[512,512]{1,0:T(8,128)(2,1)} %w_ref.1, ...), custom_call_target="tpu_custom_call" | custom-call | tf_op jit(solution)/shard_map/pallas_call | solution.py:508
  76.7 0.0 copy-start
  76.7 1.9 %copy.14 = bf16[256,1024]{1,0:T(8,128)(2,1)} copy(bf16[256,1024]{1,0:T(8,128)(2,1)} %get-tuple-element.8) | data formatting | bytes 1048576
  78.6 0.0 copy-done
  78.7 0.0 copy-start.2
  78.7 0.7 copy.15
  79.4 0.2 copy-done.2
  79.5 0.0 copy-start.1
  79.5 0.6 copy.16
  80.1 0.2 copy-done.1
  80.4 0.6 copy.17
Async XLA Ops:
  76.7 1.9 %copy-start = (bf16[256,512]{1,0:T(8,128)(2,1)S(1)}, bf16[256,512]{1,0:T(8,128)(2,1)}, u32[]{:S(2)}) copy-start(bf16[256,512]{1,0:T(8,128)(2,1)} %get-tuple-element.9) | copy-start | bytes 786436
  78.7 0.9 %copy-start.2 = (bf16[256,128]{1,0:T(8,128)(2,1)S(1)}, bf16[256,128]{1,0:T(8,128)(2,1)}, u32[]{:S(2)}) copy-start(bf16[256,128]{1,0:T(8,128)(2,1)} %get-tuple-element.10) | copy-start | bytes 196612
  79.5 0.9 %copy-start.1 = (bf16[256,128]{1,0:T(8,128)(2,1)S(1)}, bf16[256,128]{1,0:T(8,128)(2,1)}, u32[]{:S(2)}) copy-start(bf16[256,128]{1,0:T(8,128)(2,1)} %get-tuple-element.11) | copy-start | bytes 196612
